TPU v7x, 128 devices: a whole 4x4x4 slice. The times are simulated.
128 devices in a mesh: dp: 64 (over x, z_lo, y, core), tensor: 2 (over z_hi).
Axes of the slice: x: 4, y: 4, z: 4 (z_hi: 2, z_lo: 2; z = z_hi * 2 + z_lo), core: 2. Of those that a mesh axis runs over, the one named last changes fastest.
Arguments:
- tokens: bfloat16 [49152, 896], P(('dp', 'tensor')), may hold values from -6 to 6
- long_count: int32 [64], P('dp'), may hold values from 0 to 1
- attn_gain: bfloat16 [896], replicated, may hold values from 0.5 to 1.5
- w_query: bfloat16 [896, 896], P(None, 'tensor'), may hold values from -0.1875 to 0.1875
- b_query: bfloat16 [896], P('tensor'), may hold values from -3 to 3
- w_key: bfloat16 [896, 128], P(None, 'tensor'), may hold values from -0.1875 to 0.1875
- b_key: bfloat16 [128], P('tensor'), may hold values from -3 to 3
- w_value: bfloat16 [896, 128], P(None, 'tensor'), may hold values from -0.1875 to 0.1875
- b_value: bfloat16 [128], P('tensor'), may hold values from -3 to 3
- w_out: bfloat16 [896, 896], P('tensor'), may hold values from -0.75 to 0.75
- mlp_gain: bfloat16 [896], replicated, may hold values from 0.5 to 1.5
- w_gate: bfloat16 [896, 4864], P(None, 'tensor'), may hold values from -0.1875 to 0.1875
- w_up: bfloat16 [896, 4864], P(None, 'tensor'), may hold values from -0.1875 to 0.1875
- w_down: bfloat16 [4864, 896], P('tensor'), may hold values from -0.078125 to 0.078125
- cotangent: bfloat16 [49152, 896], P(('dp', 'tensor')), may hold values from -6 to 6
Outputs:
- output: bfloat16 [49152, 896], P(('dp', 'tensor'))
- grad_tokens: bfloat16 [49152, 896], P(('dp', 'tensor'))
- grad_attn_gain: float32 [896], replicated
- grad_w_query: float32 [896, 896], P(None, 'tensor')
- grad_b_query: float32 [896], P('tensor')
- grad_w_key: float32 [896, 128], P(None, 'tensor')
- grad_b_key: float32 [128], P('tensor')
- grad_w_value: float32 [896, 128], P(None, 'tensor')
- grad_b_value: float32 [128], P('tensor')
- grad_w_out: float32 [896, 896], P('tensor')
- grad_mlp_gain: float32 [896], replicated
- grad_w_gate: float32 [896, 4864], P(None, 'tensor')
- grad_w_up: float32 [896, 4864], P(None, 'tensor')
- grad_w_down: float32 [4864, 896], P('tensor')
Inputs may be any that keep to these rules, and one draw needn't show every extreme that they name: `long_count`: 1 where the group holds a sequence of 512 tokens followed by one of 256; 0 where it holds three sequences of 256.
All inputs are finite; a program needn't handle non-finite values.
Results may differ from a plain program's by a relative error of at most 0.025.
Values may be sent and summed in bfloat16 or wider, within the bound.
No kernel may reach another device: no remote copies, remote signals or barrier semaphores. Data moves between devices by JAX's collectives and lax.ppermute only.
A program may use at most 192 MiB of HBM per device.

v0:
```python
import math

import jax
import jax.numpy as jnp
from jax import lax
from jax.sharding import PartitionSpec as P

HD = 64


EPSILON = 1e-06
ROPE_BASE = 1000000.0


def normalize(field):
    factor = lax.rsqrt(jnp.mean(field * field, axis=-1, keepdims=True) + EPSILON)
    return (field * factor, factor)


def norm_back(grad_normed, normed, factor, gain):
    scaled = grad_normed * gain
    return factor * (scaled - normed * jnp.mean(scaled * normed, axis=-1, keepdims=True))


def rotate(field, cosine, sine):
    halfway = field.shape[-1] // 2
    first_half = field[..., :halfway]
    second_half = field[..., halfway:]
    return jnp.concatenate(
        [first_half * cosine - second_half * sine, second_half * cosine + first_half * sine],
        axis=-1,
    )


def dot_first(left, right):
    return lax.dot_general(
        left, right, (((0,), (0,)), ((), ())), preferred_element_type=jnp.float32
    )


def dot_last(left, right):
    return lax.dot_general(
        left, right, (((1,), (1,)), ((), ())), preferred_element_type=jnp.float32
    )


def layout(long_count, group_rows):
    short_len = group_rows // 3
    row_index = jnp.arange(group_rows, dtype=jnp.int32)
    is_long = long_count[0] == 1
    second = (row_index >= 2 * short_len).astype(jnp.int32)
    segment = jnp.where(is_long, second, row_index // short_len)
    offset = jnp.where(is_long, second * 2 * short_len, row_index // short_len * short_len)
    position = (row_index - offset).astype(jnp.float32)
    freq_index = jnp.arange(HD // 2, dtype=jnp.float32)
    inverse = ROPE_BASE ** (-2.0 * freq_index / HD)
    angle = position[:, None] * inverse[None, :]
    allowed = (segment[:, None] == segment[None, :]) & (row_index[None, :] <= row_index[:, None])
    return (jnp.cos(angle)[:, None, :], jnp.sin(angle)[:, None, :], allowed)


def shards(
    tokens,
    long_count,
    attn_gain,
    w_query,
    b_query,
    w_key,
    b_key,
    w_value,
    b_value,
    w_out,
    mlp_gain,
    w_gate,
    w_up,
    w_down,
    cotangent,
):
    resid = tokens.astype(jnp.float32)
    gain_one = attn_gain.astype(jnp.float32)
    gain_two = mlp_gain.astype(jnp.float32)
    normed_one, factor_one = normalize(resid)
    attn_in = lax.all_gather(
        (normed_one * gain_one).astype(jnp.bfloat16), "tensor", axis=0, tiled=True
    )
    group_rows = attn_in.shape[0]
    cosine, sine, allowed = layout(long_count, group_rows)
    q_heads = w_query.shape[1] // HD
    kv_heads = w_key.shape[1] // HD
    per_group = q_heads // kv_heads
    scale = 1.0 / math.sqrt(HD)
    query_lin = jnp.dot(attn_in, w_query, preferred_element_type=jnp.float32) + b_query.astype(
        jnp.float32
    )
    key_lin = jnp.dot(attn_in, w_key, preferred_element_type=jnp.float32) + b_key.astype(
        jnp.float32
    )
    value_lin = jnp.dot(attn_in, w_value, preferred_element_type=jnp.float32) + b_value.astype(
        jnp.float32
    )
    queries = rotate(query_lin.reshape(group_rows, q_heads, HD), cosine, sine).astype(jnp.bfloat16)
    queries = queries.reshape(group_rows, kv_heads, per_group, HD)
    keys = rotate(key_lin.reshape(group_rows, kv_heads, HD), cosine, sine).astype(jnp.bfloat16)
    values = value_lin.reshape(group_rows, kv_heads, HD).astype(jnp.bfloat16)

    def masked_scores():
        scored = (
            jnp.einsum("qcgd,kcd->cgqk", queries, keys, preferred_element_type=jnp.float32) * scale
        )
        return jnp.where(allowed, scored, -1e30)

    scores = masked_scores()
    summit = jnp.max(scores, axis=-1, keepdims=True)
    expo = jnp.exp(scores - summit)
    total = jnp.sum(expo, axis=-1, keepdims=True)
    chance = expo / total
    log_total = summit + jnp.log(total)
    attended = jnp.einsum(
        "cgqk,kcd->qcgd", chance.astype(jnp.bfloat16), values, preferred_element_type=jnp.float32
    )
    attended = attended.reshape(group_rows, q_heads * HD).astype(jnp.bfloat16)
    picked = attended
    hidden_mid = resid + lax.psum_scatter(
        jnp.dot(picked, w_out, preferred_element_type=jnp.float32),
        "tensor",
        scatter_dimension=0,
        tiled=True,
    )
    normed_two, factor_two = normalize(hidden_mid)
    mlp_in = lax.all_gather(
        (normed_two * gain_two).astype(jnp.bfloat16), "tensor", axis=0, tiled=True
    )
    gate_val = jnp.dot(mlp_in, w_gate, preferred_element_type=jnp.float32)
    up_val = jnp.dot(mlp_in, w_up, preferred_element_type=jnp.float32)
    sigmoid_gate = jax.nn.sigmoid(gate_val)
    active = (gate_val * sigmoid_gate * up_val).astype(jnp.bfloat16)
    picked = active
    output = (
        hidden_mid
        + lax.psum_scatter(
            jnp.dot(picked, w_down, preferred_element_type=jnp.float32).astype(jnp.bfloat16),
            "tensor",
            scatter_dimension=0,
            tiled=True,
        ).astype(jnp.float32)
    ).astype(jnp.bfloat16)
    grad_out_rows = lax.all_gather(cotangent, "tensor", axis=0, tiled=True)
    grad_active = dot_last(grad_out_rows, w_down)
    grad_w_down = dot_first(active, grad_out_rows)
    grad_gate = (
        grad_active * up_val * sigmoid_gate * (1.0 + gate_val * (1.0 - sigmoid_gate))
    ).astype(jnp.bfloat16)
    grad_up = (grad_active * gate_val * sigmoid_gate).astype(jnp.bfloat16)
    grad_w_gate = dot_first(mlp_in, grad_gate)
    grad_w_up = dot_first(mlp_in, grad_up)
    grad_mlp_in = lax.psum_scatter(
        dot_last(grad_gate, w_gate) + dot_last(grad_up, w_up),
        "tensor",
        scatter_dimension=0,
        tiled=True,
    )
    grad_gain_two = jnp.sum(grad_mlp_in * normed_two, axis=0)
    grad_mid = cotangent.astype(jnp.float32) + norm_back(
        grad_mlp_in, normed_two, factor_two, gain_two
    )
    grad_branch = lax.all_gather(grad_mid.astype(jnp.bfloat16), "tensor", axis=0, tiled=True)
    grad_w_out = dot_first(attended, grad_branch)
    grad_attended = dot_last(grad_branch, w_out).astype(jnp.bfloat16)
    grad_attended = grad_attended.reshape(group_rows, kv_heads, per_group, HD)
    chance = jnp.exp(masked_scores() - log_total)
    chance_low = chance.astype(jnp.bfloat16)
    grad_values = jnp.einsum(
        "cgqk,qcgd->kcd", chance_low, grad_attended, preferred_element_type=jnp.float32
    )
    grad_chance = jnp.einsum(
        "qcgd,kcd->cgqk", grad_attended, values, preferred_element_type=jnp.float32
    )
    inner = jnp.sum(chance * grad_chance, axis=-1, keepdims=True)
    grad_scores = (chance * (grad_chance - inner)).astype(jnp.bfloat16)
    grad_queries = (
        jnp.einsum("cgqk,kcd->qcgd", grad_scores, keys, preferred_element_type=jnp.float32) * scale
    )
    grad_keys = (
        jnp.einsum("cgqk,qcgd->kcd", grad_scores, queries, preferred_element_type=jnp.float32)
        * scale
    )
    grad_q_lin = rotate(grad_queries.reshape(group_rows, q_heads, HD), cosine, -sine)
    grad_q_lin = grad_q_lin.reshape(group_rows, q_heads * HD).astype(jnp.bfloat16)
    grad_k_lin = (
        rotate(grad_keys, cosine, -sine).reshape(group_rows, kv_heads * HD).astype(jnp.bfloat16)
    )
    grad_v_lin = grad_values.reshape(group_rows, kv_heads * HD).astype(jnp.bfloat16)
    grad_w_query = dot_first(attn_in, grad_q_lin)
    grad_w_key = dot_first(attn_in, grad_k_lin)
    grad_w_value = dot_first(attn_in, grad_v_lin)
    grad_b_query = jnp.sum(grad_q_lin.astype(jnp.float32), axis=0)
    grad_b_key = jnp.sum(grad_k_lin.astype(jnp.float32), axis=0)
    grad_b_value = jnp.sum(grad_v_lin.astype(jnp.float32), axis=0)
    grad_attn_in = lax.psum_scatter(
        (
            dot_last(grad_q_lin, w_query)
            + dot_last(grad_k_lin, w_key)
            + dot_last(grad_v_lin, w_value)
        ).astype(jnp.bfloat16),
        "tensor",
        scatter_dimension=0,
        tiled=True,
    ).astype(jnp.float32)
    grad_gain_one = jnp.sum(grad_attn_in * normed_one, axis=0)
    grad_tokens = (grad_mid + norm_back(grad_attn_in, normed_one, factor_one, gain_one)).astype(
        jnp.bfloat16
    )
    every_total = lax.psum(
        (
            grad_w_query,
            grad_b_query,
            grad_w_key,
            grad_b_key,
            grad_w_value,
            grad_b_value,
            grad_w_out,
            grad_gain_one,
            grad_w_gate,
            grad_w_up,
            grad_w_down,
            grad_gain_two,
        ),
        "dp",
    )
    (
        grad_w_query,
        grad_b_query,
        grad_w_key,
        grad_b_key,
        grad_w_value,
        grad_b_value,
        grad_w_out,
        grad_gain_one,
        grad_w_gate,
        grad_w_up,
        grad_w_down,
        grad_gain_two,
    ) = every_total
    grad_gain_one, grad_gain_two = lax.psum((grad_gain_one, grad_gain_two), "tensor")
    return (
        output,
        grad_tokens,
        grad_gain_one,
        grad_w_query,
        grad_b_query,
        grad_w_key,
        grad_b_key,
        grad_w_value,
        grad_b_value,
        grad_w_out,
        grad_gain_two,
        grad_w_gate,
        grad_w_up,
        grad_w_down,
    )


def solution(mesh):
    placed = (
        P(("dp", "tensor"), None),
        P("dp"),
        P(),
        P(None, "tensor"),
        P("tensor"),
        P(None, "tensor"),
        P("tensor"),
        P(None, "tensor"),
        P("tensor"),
        P("tensor", None),
        P(),
        P(None, "tensor"),
        P(None, "tensor"),
        P("tensor", None),
        P(("dp", "tensor"), None),
    )
    return jax.shard_map(
        shards,
        mesh=mesh,
        in_specs=placed,
        out_specs=(
            P(("dp", "tensor"), None),
            P(("dp", "tensor"), None),
            P(),
            P(None, "tensor"),
            P("tensor"),
            P(None, "tensor"),
            P("tensor"),
            P(None, "tensor"),
            P("tensor"),
            P("tensor", None),
            P(),
            P(None, "tensor"),
            P(None, "tensor"),
            P("tensor", None),
        ),
        check_vma=False,
    )
```

profile of v0, /device:TPU:1, one launch (start us, length us, event | category | flops | bytes accessed | tf_op | source)
XLA Modules:
  0.0 1055.3 jit_solution(2419565446134901867)
XLA Ops:
  15.2 28.9 %all-gather.5.cloned.1.call-done = bf16[768,896]{1,0:T(8,128)(2,1)} async-done(((bf16[384,896]{1,0:T(8,128)(2,1)}), bf16[768,896]{1,0:T(8,128)(2,1)}) %all-gather.5.cloned.1.call-update) | async-done | bytes 1376272 | tf_op jit(solution)/shard_map/all_gather | solution.py:83
  49.8 7.2 fusion.79
  57.1 8.0 fusion.3
  65.7 7.4 fusion.26
  76.9 41.3 %reduce-scatter.5.cloned.1.call-done = f32[384,896]{1,0:T(8,128)} async-done(((f32[768,896]{1,0:T(8,128)}), f32[384,896]{1,0:T(8,128)}) %reduce-scatter.5.cloned.1.call-update) | async-done | bytes 1376272 | tf_op jit(solution)/shard_map/reduce_scatter | solution.py:123
  122.5 27.7 %all-gather.7.cloned.1.call-done = bf16[768,896]{1,0:T(8,128)(2,1)} async-done(((bf16[384,896]{1,0:T(8,128)(2,1)}), bf16[768,896]{1,0:T(8,128)(2,1)}) %all-gather.7.cloned.1.call-update) | async-done | bytes 1376272 | tf_op jit(solution)/shard_map/all_gather | solution.py:130
  150.2 10.0 fusion.81
  160.2 8.7 fusion.82
  169.0 11.3 %all-gather.9.cloned.1.call-done = bf16[768,896]{1,0:T(8,128)(2,1)} async-done(((bf16[384,896]{1,0:T(8,128)(2,1)}), bf16[768,896]{1,0:T(8,128)(2,1)}) %all-gather.9.cloned.1.call-update) | async-done | bytes 1376272 | tf_op jit(solution)/shard_map/all_gather | solution.py:147
  180.2 12.9 %multiply_convert_fusion = (bf16[768,2432]{1,0:T(8,128)(2,1)S(1)}, bf16[768,2432]{1,0:T(8,128)(2,1)S(1)}, bf16[768,2432]{1,0:T(8,128)(2,1)}) fusion(f32[768,2432]{1,0:T(8,128)} %fusion.81, f32[768,2432]{1,0:T(8,128)} %fusion.82, bf16[768,896]{1,0:T(8,128)(2,1)} %all-gather.9.cloned.1.call-done, bf16[2432,896]{1,0:T(8,128)(2,1)} %param.28), kind=kOutput, calls=%fused_computation.17 | convolution fusion | flops 3376939008 | bytes 31883264 | tf_op jit(solution)/shard_map/dot_general | solution.py:42
  193.1 9.1 fusion.83
  202.2 8.0 convolution_add_fusion
  210.7 42.1 %reduce-scatter.9.cloned.1.call-done = f32[384,896]{1,0:T(8,128)} async-done(((f32[768,896]{1,0:T(8,128)}), f32[384,896]{1,0:T(8,128)}) %reduce-scatter.9.cloned.1.call-update) | async-done | bytes 1376272 | tf_op jit(solution)/shard_map/reduce_scatter | solution.py:156
  258.6 27.1 %all-gather.11.cloned.1.call-done = bf16[768,896]{1,0:T(8,128)(2,1)} async-done(((bf16[384,896]{1,0:T(8,128)(2,1)}), bf16[768,896]{1,0:T(8,128)(2,1)}) %all-gather.11.cloned.1.call-update) | async-done | bytes 1376272 | tf_op jit(solution)/shard_map/all_gather | solution.py:166
  288.1 13.1 %fusion = (f32[7,768]{1,0:T(8,128)S(1)}, f32[768,768,7]{1,0,2:T(8,128)}) fusion(f32[1,7,768,768]{2,3,1,0:T(8,128)} %get-tuple-element.53, f32[7,768]{1,0:T(8,128)S(1)} %copy-done.38, bf16[768,64,1]{0,1,2:T(8,128)(2,1)S(1)} %copy-done.35, bf16[768,7,64]{0,2,1:T(8,128)(2,1)S(1)} %bitcast.144), kind=kOutput, calls=%fused_computation.3 | convolution fusion | flops 540863232 | bytes 33859584 | tf_op jit(solution)/shard_map/qcgd,kcd->cgqk/dot_general | solution.py:175
  304.2 7.8 fusion.8
  327.6 8.6 convolution_convert_fusion
  336.3 9.9 fusion.86
  346.2 6.1 fusion.87
  352.3 6.3 fusion.88
  368.7 274.1 %all-reduce = (f32[896]{0:T(1024)S(1)}, f32[448]{0:T(512)}, f32[64]{0:T(128)}, f32[64]{0:T(128)}, f32[896]{0:T(1024)S(1)}) all-reduce(f32[896]{0:T(1024)S(1)} %get-tuple-element.16, f32[448]{0:T(512)} %reduce_sum.109, f32[64]{0:T(128)} %convert_reduce_fusion.2, ...), channel_id=1, replica_groups=mesh['dp'=64,'tensor'=2] {'dp'}, use_global_device_ids=true, to_apply=%region_12.13 | all-reduce | flops 2368 | bytes 18944 | tf_op jit(solution)/shard_map/psum | solution.py:213
  642.8 6.4 all-reduce.2
  652.6 372.4 %all-reduce.5.cloned.1.call-done = (f32[896,448]{0,1:T(8,128)}, f32[896,64]{0,1:T(8,128)}, f32[896,64]{0,1:T(8,128)}, f32[448,896]{1,0:T(8,128)}, f32[896,2432]{...) async-done(((f32[896,448]{0,1:T(8,128)}, f32[896,64]{0,1:T(8,128)}, f32[896,64]{0,1:T(8,128)}, f32[448,896]{1,0:T(8,128)}, f32[896,2432]{1,0:T(8,128)}, ...) | async-done | bytes 29818896 | tf_op jit(solution)/shard_map/psum | solution.py:213
  1030.4 8.6 copy.49
  (226 shorter events, 76.9 us)
Async XLA Ops:
  7.2 65.9 %copy-start = (bf16[448,896]{1,0:T(8,128)(2,1)S(1)}, bf16[448,896]{1,0:T(8,128)(2,1)}, u32[]{:S(2)}) copy-start(bf16[448,896]{1,0:T(8,128)(2,1)} %param.24) | copy-start | bytes 2408452
  7.2 36.9 %all-gather.5.cloned.1.call-start = ((), (), s32[]{:S(2)}) async-start(), calls=%async_computation.4 | async-start | bytes 2064384 | tf_op jit(solution)/shard_map/all_gather | solution.py:83
  9.3 34.8 %copy-start.32 = (bf16[896,64]{0,1:T(8,128)(2,1)S(1)}, bf16[896,64]{0,1:T(8,128)(2,1)}, u32[]{:S(2)}) copy-start(bf16[896,64]{0,1:T(8,128)(2,1)} %param.20) | copy-start | bytes 344068
  9.3 36.8 %copy-start.57 = (f32[384]{0:T(512)}, f32[384]{0:T(512)S(1)}, u32[]{:S(2)}) copy-start(f32[384]{0:T(512)S(1)} %add_rsqrt_fusion.1) | copy-start | bytes 4612
  11.6 106.6 %reduce-scatter.5.cloned.1.call-start = ((), (), s32[]{:S(2)}) async-start(), calls=%async_computation.5 | async-start | bytes 4128768 | tf_op jit(solution)/shard_map/reduce_scatter | solution.py:123
  12.9 33.7 %copy-start.60 = (f32[32]{0:T(128)}, f32[32]{0:T(128)S(1)}, u32[]{:S(2)}) copy-start(f32[32]{0:T(128)S(1)} %multiply_power_fusion) | copy-start | bytes 388
  12.9 33.7 %copy-start.50 = (f32[768]{0:T(1024)}, f32[768]{0:T(1024)S(1)}, u32[]{:S(2)}) copy-start(f32[768]{0:T(1024)S(1)} %get-tuple-element.59) | copy-start | bytes 9220
  14.0 34.8 %copy-start.20 = (f32[768,32]{0,1:T(8,128)}, f32[768,32]{0,1:T(8,128)S(1)}, u32[]{:S(2)}) copy-start(f32[768,32]{0,1:T(8,128)S(1)} %get-tuple-element.51) | copy-start | bytes 294916
  75.7 74.5 %all-gather.7.cloned.1.call-start = ((), (), s32[]{:S(2)}) async-start(), calls=%async_computation.6 | async-start | bytes 2064384 | tf_op jit(solution)/shard_map/all_gather | solution.py:130
  121.7 58.6 %all-gather.9.cloned.1.call-start = ((), (), s32[]{:S(2)}) async-start(), calls=%async_computation.8 | async-start | bytes 2064384 | tf_op jit(solution)/shard_map/all_gather | solution.py:147
  122.3 130.5 %reduce-scatter.9.cloned.1.call-start = ((), (), s32[]{:S(2)}) async-start(), calls=%async_computation.9 | async-start | bytes 4128768 | tf_op jit(solution)/shard_map/reduce_scatter | solution.py:156
  210.2 75.5 %all-gather.11.cloned.1.call-start = ((), (), s32[]{:S(2)}) async-start(), calls=%async_computation.10 | async-start | bytes 2064384 | tf_op jit(solution)/shard_map/all_gather | solution.py:166
  257.2 109.8 %reduce-scatter.11.cloned.1.call-start = ((), (), s32[]{:S(2)}) async-start(), calls=%async_computation.11 | async-start | bytes 2064384 | tf_op jit(solution)/shard_map/reduce_scatter | solution.py:199
  288.0 13.2 %slice-start = ((s8[16515072]{0:T(1024)(128)(4,1)}), s8[4194304]{0:T(1024)(128)(4,1)S(1)}, s32[]{:S(2)}) async-start(s8[16515072]{0:T(1024)(128)(4,1)} %bitcast.138), calls=%async_computation.13 | async-start | bytes 8388608
  288.1 13.2 %slice-start.1 = ((s8[16515072]{0:T(1024)(128)(4,1)}), s8[4194304]{0:T(1024)(128)(4,1)S(1)}, s32[]{:S(2)}) async-start(s8[16515072]{0:T(1024)(128)(4,1)} %bitcast.138), calls=%async_computation.14 | async-start | bytes 8388608
  288.1 15.1 %slice-start.2 = ((s8[16515072]{0:T(1024)(128)(4,1)}), s8[4194304]{0:T(1024)(128)(4,1)S(1)}, s32[]{:S(2)}) async-start(s8[16515072]{0:T(1024)(128)(4,1)} %bitcast.138), calls=%async_computation.15 | async-start | bytes 8388608
  288.1 16.2 %slice-start.3 = ((s8[16515072]{0:T(1024)(128)(4,1)}), s8[3932160]{0:T(1024)(128)(4,1)S(1)}, s32[]{:S(2)}) async-start(s8[16515072]{0:T(1024)(128)(4,1)} %bitcast.138), calls=%async_computation.16 | async-start | bytes 7864320
  327.4 321.9 %reduce-scatter.7.cloned.1.call-start = ((), (), s32[]{:S(2)}) async-start(), calls=%async_computation.7 | async-start | bytes 2064384 | tf_op jit(solution)/shard_map/reduce_scatter | solution.py:140
  336.2 688.8 %all-reduce.5.cloned.1.call-start = ((), (), s32[]{:S(2)}) async-start(), calls=%async_computation.12 | async-start | bytes 59637760 | tf_op jit(solution)/shard_map/psum | solution.py:213
  364.8 284.4 %copy-start.47 = (f32[896]{0:T(1024)S(1)}, f32[896]{0:T(1024)}, u32[]{:S(2)}) copy-start(f32[896]{0:T(1024)} %convert_element_type.159) | copy-start | bytes 10756
  364.8 284.4 %copy-start.56 = (f32[384]{0:T(512)S(1)}, f32[384]{0:T(512)}, u32[]{:S(2)}) copy-start(f32[384]{0:T(512)} %copy-done.54) | copy-start | bytes 4612
  364.8 284.4 %copy-start.5 = (f32[384,896]{1,0:T(8,128)S(1)}, f32[384,896]{1,0:T(8,128)}, u32[]{:S(2)}) copy-start(f32[384,896]{1,0:T(8,128)} %reduce-scatter.9.cloned.1.call-done) | copy-start | bytes 4128772
  1030.4 13.0 %slice-start.4 = ((s8[8716288]{0:T(1024)(128)(4,1)}), s8[4194304]{0:T(1024)(128)(4,1)S(1)}, s32[]{:S(2)}) async-start(s8[8716288]{0:T(1024)(128)(4,1)} %bitcast.140), calls=%async_computation.17 | async-start | bytes 8388608
  1030.4 14.6 %slice-start.5 = ((s8[8716288]{0:T(1024)(128)(4,1)}), s8[4194304]{0:T(1024)(128)(4,1)S(1)}, s32[]{:S(2)}) async-start(s8[8716288]{0:T(1024)(128)(4,1)} %bitcast.140), calls=%async_computation.18 | async-start | bytes 8388608
  (62 other events, 265.3 us)
Sparse Core Ops, SparseCore 0:
  11.7 32.3 all-gather.4
  75.8 42.3 reduce-scatter.4
  121.8 28.3 all-gather.6
  151.8 28.3 all-gather.8
  210.4 42.3 reduce-scatter.8
  257.3 28.3 all-gather.10
  327.5 27.2 reduce-scatter.10
  357.3 27.4 reduce-scatter.6
  389.0 635.9 all-reduce.4
where the time goes:
time: 1060 us
  waiting for transfers between devices  551 us (52%)
  blocking collectives  281 us (27%)
  matrix products  135 us (13%)
  other arithmetic  40.5 us (4%)
  local copies, waits for them, and re-layouts  31.6 us (3%)
  between operations  15.4 us (1%)
    psum x1, waiting for transfers between devices, shards(): lax.psum((grad_w_query, grad_b_query, grad_w_key, grad_b_key, grad_w_valu...  372 us
    psum x1, blocking collectives, shards(): lax.psum((grad_w_query, grad_b_query, grad_w_key, grad_b_key, grad_w_valu...  274 us
    reduce_scatter x1, waiting for transfers between devices, shards(): lax.psum_scatter(dot_last(grad_gate, w_gate) + dot_last(grad_up, w_up), '...  42.1 us
    reduce_scatter x1, waiting for transfers between devices, shards(): lax.psum_scatter(jnp.dot(picked, w_out, preferred_element_type=jnp.float3...  41.3 us
    dot_general x7, matrix products, dot_last(): lax.dot_general(left, right, (((1,), (1,)), ((), ())), preferred_element_...  35.4 us
    unnamed x161, local copies, waits for them, and re-layouts  30.1 us
    all_gather x1, waiting for transfers between devices, shards(): lax.all_gather((normed_one * gain_one).astype(jnp.bfloat16), 'tensor', ax...  28.9 us
    dot_general x7, matrix products, dot_first(): lax.dot_general(left, right, (((0,), (0,)), ((), ())), preferred_element_...  28.4 us
  transfers between devices with their start and end apart: 9, of which 7 were waited for; matrix products, arithmetic and copies ran while one was open for 6% of the time, Pallas kernels for 0%

commit v1 on v0

v1 whole, which is shorter than its diff:
```python
import functools

import jax
import jax.numpy as jnp
from jax import lax
from jax.experimental import pallas as pl
from jax.experimental.pallas import tpu as pltpu
from jax.sharding import Mesh
from jax.sharding import PartitionSpec as P

HD = 64
EPSILON = 1e-06
ROPE_BASE = 1000000.0
BF = jnp.bfloat16
F32 = jnp.float32

D = 896
HALF = 384
ROWS = 768
HEADS = 7
PIECE = 56
SLAB = 224
HID = 1280
STEP = 1152
CHUNK = 256
MIB = 1024 * 1024

VM = pl.BlockSpec(memory_space=pltpu.VMEM)
SM = pl.BlockSpec(memory_space=pltpu.SMEM)


def sds(shape, dtype):
    return jax.ShapeDtypeStruct(shape, dtype)


def nn(a, b):
    return lax.dot_general(a, b, (((1,), (0,)), ((), ())), preferred_element_type=F32)


def nt(a, b):
    return lax.dot_general(a, b, (((1,), (1,)), ((), ())), preferred_element_type=F32)


def tn(a, b):
    return lax.dot_general(a, b, (((0,), (0,)), ((), ())), preferred_element_type=F32)


def factor_of(field):
    return lax.rsqrt(jnp.mean(field * field, axis=-1, keepdims=True) + EPSILON)


def params(mib):
    return pltpu.CompilerParams(vmem_limit_bytes=mib * MIB)


def cost(flops, size, trans=0):
    return pl.CostEstimate(flops=flops, bytes_accessed=size, transcendentals=trans)


def half_offsets(place):
    mine = pl.multiple_of(place * HALF, HALF)
    other = pl.multiple_of((1 - place) * HALF, HALF)
    return mine, other


def masks(is_long):
    row = lax.broadcasted_iota(jnp.int32, (256, 256), 0)
    col = lax.broadcasted_iota(jnp.int32, (256, 256), 1)
    causal = jnp.where(col <= row, 0.0, -1e30).astype(F32)
    before = jnp.full((256, 256), jnp.where(is_long == 1, 0.0, -1e30).astype(F32))
    return causal, jnp.concatenate([before, causal], axis=1)


SPANS = ((0, 0, 256), (256, 0, 512), (512, 512, 768))


def attention_kernel(info, tok_own, tok_rec, gain, w_all, b_all, cosine, sine,
                     attn_in, rotated, value, stats, att_send, att_keep):
    mine, other = half_offsets(info[0])
    for src, off in ((tok_own, mine), (tok_rec, other)):
        field = src[...].astype(F32)
        attn_in[pl.ds(off, HALF), :] = (field * factor_of(field) * gain[...]).astype(BF)
    for block in range(3):
        rows = slice(256 * block, 256 * block + 256)
        lin = nn(attn_in[rows, :], w_all[...]) + b_all[...]
        cos_b, sin_b = cosine[rows, :], sine[rows, :]
        for head in range(HEADS + 1):
            part = lin[:, 128 * head : 128 * head + 128]
            turned = part * cos_b + pltpu.roll(part, 64, 1) * sin_b
            rotated[rows, 128 * head : 128 * head + 128] = turned.astype(BF)
        value[rows, :] = lin[:, 1024:1152].astype(BF)
    causal, wide = masks(info[1])
    lane = lax.broadcasted_iota(jnp.int32, (256, 128), 1)
    for block, (first, low, high) in enumerate(SPANS):
        rows = slice(first, first + 256)
        mask = wide if block == 1 else causal
        keys = rotated[low:high, 1024 - 128 :]
        vals = value[low:high, :]
        kept = jnp.zeros((256, 128), F32)
        outs = []
        for head in range(HEADS):
            scores = nt(rotated[rows, 128 * head : 128 * head + 128], keys) * 0.0625 + mask
            top = jnp.max(scores, axis=-1, keepdims=True)
            expo = jnp.exp(scores - top)
            total = jnp.sum(expo, axis=-1, keepdims=True)
            kept = jnp.where(lane == head, top + jnp.log(total), kept)
            outs.append(nn(expo.astype(BF), vals) * (1.0 / total))
        stats[rows, :] = kept
        outs.append(jnp.zeros((256, 128), F32))
        for pair in range(4):
            both = jnp.where(lane < 64, outs[2 * pair], outs[2 * pair + 1]).astype(BF)
            att_keep[rows, 128 * pair : 128 * pair + 128] = both
            if pair < 3:
                att_send[rows, 128 * pair : 128 * pair + 128] = both
            else:
                att_send[rows, 384:448] = both[:, :64]


def attention(info, tok_own, tok_rec, gain, w_all, b_all, cosine, sine):
    return pl.pallas_call(
        attention_kernel,
        name="attention_forward",
        in_specs=[SM] + [VM] * 7,
        out_specs=[VM] * 6,
        out_shape=[
            sds((ROWS, D), BF),
            sds((ROWS, 1024), BF),
            sds((ROWS, 128), BF),
            sds((ROWS, 128), F32),
            sds((ROWS, 448), BF),
            sds((ROWS, 512), BF),
        ],
        compiler_params=params(48),
        cost_estimate=cost(4 * 10**9, 12 * 10**6, 3 * 10**6),
    )(info, tok_own, tok_rec, gain, w_all, b_all, cosine, sine)


def project_kernel(info, att_own, att_rec, wo_own, wo_rec, tok_own, tok_rec, gain, hidden, mlp_in):
    mine, other = half_offsets(info[0])
    for src, off in ((tok_own, mine), (tok_rec, other)):
        rows = pl.ds(off, HALF)
        field = (
            nn(att_own[rows, :], wo_own[...]) + nn(att_rec[rows, :], wo_rec[...])
        ) + src[...].astype(F32)
        hidden[rows, :] = field
        mlp_in[rows, :] = (field * factor_of(field) * gain[...]).astype(BF)


def project(info, att_own, att_rec, wo_own, wo_rec, tok_own, tok_rec, gain):
    return pl.pallas_call(
        project_kernel,
        name="project_norm",
        in_specs=[SM] + [VM] * 7,
        out_specs=[VM] * 2,
        out_shape=[sds((ROWS, D), F32), sds((ROWS, D), BF)],
        compiler_params=params(40),
        cost_estimate=cost(13 * 10**8, 10 * 10**6),
    )(info, att_own, att_rec, wo_own, wo_rec, tok_own, tok_rec, gain)


def turn_kernel(info, own, rec, by_x, by_y):
    for at, src in enumerate((own, rec)):
        cols = slice(ROWS * at, ROWS * at + ROWS)
        for slab in range(4):
            turned = src[:, SLAB * slab : SLAB * slab + SLAB].astype(F32).T.astype(BF)
            for place, out in ((info[2], by_x), (info[3], by_y)):
                slot = lax.rem(slab - place + 4, 4)
                out[pl.ds(pl.multiple_of(slot * SLAB, SLAB), SLAB), cols] = turned


def turn(info, own, rec):
    return pl.pallas_call(
        turn_kernel,
        name="transpose_rows",
        in_specs=[SM] + [VM] * 2,
        out_specs=[VM] * 2,
        out_shape=[sds((D, 2 * ROWS), BF)] * 2,
        compiler_params=params(48),
        cost_estimate=cost(10**6, 8 * 10**6),
    )(info, own, rec)


def feed_kernel(first, lanes, m_own, m_rec, g_own, g_rec, m_x, m_y, g_t, wg, wu, wd, *rest):
    rest = list(rest)
    starts = [rest.pop(0) for _ in range(0 if first else 4)]
    slots_x = [rest.pop(0) for _ in range(4)]
    slots_y = [rest.pop(0) for _ in range(4)]
    ends = [rest.pop(0) for _ in range(4)]
    act_s, gate_s, up_s, *sums = rest
    step = pl.program_id(0)

    @pl.when(step == 0)
    def _():
        for at in range(4):
            sums[at][...] = jnp.zeros((ROWS, D), F32) if first else starts[at][...].astype(F32)

    for at, (m, g) in enumerate(((m_own, g_own), (m_rec, g_rec))):
        rows = slice(ROWS * at, ROWS * at + ROWS)
        gate = nn(m[...], wg[...])
        up = nn(m[...], wu[...])
        grad = nt(g[...], wd[...])
        sig = 1.0 / (1.0 + jnp.exp(-gate))
        swish = gate * sig
        act_s[rows, :] = (swish * up).astype(BF)
        up_s[rows, :] = (grad * swish).astype(BF)
        gate_s[rows, :] = (grad * up * (sig + swish * (1.0 - sig))).astype(BF)
        sums[at][...] += nn(act_s[rows, :], wd[...])
        sums[2 + at][...] += nt(gate_s[rows, :], wg[...]) + nt(up_s[rows, :], wu[...])
    at_x = pl.ds(pl.multiple_of(step * CHUNK, CHUNK), CHUNK)
    at_down = pl.ds(pl.multiple_of(step * CHUNK + lanes, CHUNK), CHUNK)
    for left, right, slots, cols in (
        (m_x, gate_s, slots_x, at_x),
        (m_y, up_s, slots_y, at_x),
        (g_t, act_s, slots_x if first else slots_y, at_down),
    ):
        product = nn(left[...], right[...])
        for slot in range(4):
            for piece in range(4):
                low = SLAB * slot + PIECE * piece
                slots[slot][piece, :, cols] = product[low : low + PIECE, :].astype(BF)

    @pl.when(step == pl.num_programs(0) - 1)
    def _():
        for at in range(4):
            ends[at][...] = sums[at][...].astype(BF)


def feed(first, m_own, m_rec, g_own, g_rec, m_x, m_y, g_t, wg, wu, wd, starts):
    steps = 3 if first else 2
    at = 0 if first else 3
    lanes = steps * CHUNK
    wide_x, wide_y = (2 * lanes, lanes) if first else (lanes, 2 * lanes)

    def whole(shape):
        zeros = (0,) * len(shape)
        return pl.BlockSpec(shape, lambda j: zeros, pipeline_mode=pl.Buffered(1))

    rows = whole((ROWS, D))
    turned = whole((D, 2 * ROWS))
    wide = pl.BlockSpec((D, CHUNK), lambda j: (0, j + at))
    tall = pl.BlockSpec((CHUNK, D), lambda j: (j + at, 0))
    return pl.pallas_call(
        functools.partial(feed_kernel, first, lanes),
        name="feed_first" if first else "feed_second",
        grid=(steps,),
        in_specs=[rows] * 4 + [turned] * 3 + [wide, wide, tall] + [rows] * len(starts),
        out_specs=[whole((4, PIECE, wide_x))] * 4 + [whole((4, PIECE, wide_y))] * 4 + [rows] * 4,
        out_shape=[sds((4, PIECE, wide_x), BF)] * 4
        + [sds((4, PIECE, wide_y), BF)] * 4
        + [sds((ROWS, D), BF)] * 4,
        scratch_shapes=[pltpu.VMEM((2 * ROWS, CHUNK), BF)] * 3 + [pltpu.VMEM((ROWS, D), F32)] * 4,
        compiler_params=params(63),
        cost_estimate=cost(steps * 63 * 10**8, 30 * 10**6, steps * 4 * 10**5),
    )(m_own, m_rec, g_own, g_rec, m_x, m_y, g_t, wg, wu, wd, *starts)


def fold_kernel(info, *refs):
    ins_x, ins_y, outs_x, outs_y = refs[:4], refs[4:8], refs[8:12], refs[12:]
    for place, ins, outs in ((info[3], ins_x, outs_x), (info[2], ins_y, outs_y)):
        for slot in range(4):
            piece = lax.rem(place + slot, 4)
            total = ins[0][piece].astype(F32)
            for ref in ins[1:]:
                total = total + ref[piece].astype(F32)
            outs[slot][...] = total.astype(BF)


def fold(info, ins_x, ins_y):
    wide_x, wide_y = ins_x[0].shape[-1], ins_y[0].shape[-1]
    return pl.pallas_call(
        fold_kernel,
        name="sum_slabs",
        in_specs=[SM] + [VM] * 8,
        out_specs=[VM] * 8,
        out_shape=[sds((PIECE, wide_x), BF)] * 4 + [sds((PIECE, wide_y), BF)] * 4,
        compiler_params=params(32),
        cost_estimate=cost(10**7, 6 * 10**6),
    )(info, *ins_x, *ins_y)


def join_kernel(*refs):
    ins_x, ins_y, out = refs[:4], refs[4:8], refs[8]
    wide = ins_x[0].shape[-1]
    for ins, cols in ((ins_x, slice(0, wide)), (ins_y, slice(wide, None))):
        total = ins[0][...].astype(F32)
        for ref in ins[1:]:
            total = total + ref[...].astype(F32)
        out[:, cols] = total.astype(BF)


def join(ins_x, ins_y):
    wide = ins_x[0].shape[-1] + ins_y[0].shape[-1]
    return pl.pallas_call(
        join_kernel,
        name="sum_pieces",
        in_specs=[VM] * 8,
        out_specs=VM,
        out_shape=sds((PIECE, wide), BF),
        compiler_params=params(16),
        cost_estimate=cost(10**6, 2 * 10**6),
    )(*ins_x, *ins_y)


def back_kernel(info, dm_own, dm_rec, cot, hidden, gain_two, tok_own, tok_rec, gain_one,
                wo_dup, att, rotated, value, stats, cosine, sine, attn_in, w_cat,
                grad_mid, da_own, da_send, pack_a, pack_b,
                branch, grad_att, lin, grad_in):
    mine, other = half_offsets(info[0])
    sum_two = jnp.zeros((1, D), F32)
    for own, off in ((True, mine), (False, other)):
        rows = pl.ds(off, HALF)
        field = hidden[rows, :]
        factor = factor_of(field)
        normed = field * factor
        grad = dm_own[rows, :].astype(F32) + dm_rec[rows, :].astype(F32)
        scaled = grad * gain_two[...]
        middle = cot[rows, :].astype(F32) + factor * (
            scaled - normed * jnp.mean(scaled * normed, axis=-1, keepdims=True)
        )
        branch[rows, :] = middle.astype(BF)
        if own:
            grad_mid[...] = middle
            sum_two = jnp.sum(grad * normed, axis=0, keepdims=True)
    grad_att[...] = nt(branch[...], wo_dup[...]).astype(BF)
    causal, wide = masks(info[1])
    lane = lax.broadcasted_iota(jnp.int32, (256, 128), 1)
    grad_k = [jnp.zeros((256, 128), F32) for _ in range(3)]
    grad_v = [jnp.zeros((256, 128), F32) for _ in range(3)]
    for block, (first, low, high) in enumerate(SPANS):
        rows = slice(first, first + 256)
        mask = wide if block == 1 else causal
        keys = rotated[low:high, 896:1024]
        vals = value[low:high, :]
        cos_b, sin_b = cosine[rows, :], sine[rows, :]
        kept = stats[rows, :]
        turned = []
        for head in range(HEADS):
            cols = slice(128 * head, 128 * head + 128)
            query, grad_o = rotated[rows, cols], grad_att[rows, cols]
            base = jnp.sum(jnp.where(lane == head, kept, 0.0), axis=-1, keepdims=True)
            chance = jnp.exp(nt(query, keys) * 0.0625 + mask - base)
            grad_p = nt(grad_o, vals) * 0.5
            inner = jnp.sum(chance * grad_p, axis=-1, keepdims=True)
            grad_s = (chance * (grad_p - inner)).astype(BF)
            low_p = chance.astype(BF)
            back = nn(grad_s, keys) * 0.125
            turned.append(back * cos_b - pltpu.roll(back, 64, 1) * sin_b)
            for at in range((high - low) // 256):
                part = slice(256 * at, 256 * at + 256)
                grad_k[low // 256 + at] += tn(grad_s[:, part], query)
                grad_v[low // 256 + at] += tn(low_p[:, part], grad_o)
        turned.append(jnp.zeros((256, 128), F32))
        for pair in range(4):
            right = pltpu.roll(turned[2 * pair + 1], 64, 1)
            lin[rows, 128 * pair : 128 * pair + 128] = jnp.where(
                lane < 64, turned[2 * pair], right
            ).astype(BF)
    for block in range(3):
        rows = slice(256 * block, 256 * block + 256)
        back = grad_k[block] * 0.125
        back = back * cosine[rows, :] - pltpu.roll(back, 64, 1) * sine[rows, :]
        back = pltpu.roll(back, 64, 1).astype(BF)
        lin[rows, 384:512] = jnp.where(lane < 64, lin[rows, 384:512], back)
        lin[rows, 512:640] = jnp.where(lane < 64, 0.0, grad_v[block]).astype(BF)
    grad_in[...] = nt(lin[...], w_cat[...])
    sum_one = jnp.zeros((1, D), F32)
    for src, out, off in ((tok_own, da_own, mine), (tok_rec, da_send, other)):
        rows = pl.ds(off, HALF)
        field = src[...].astype(F32)
        grad = grad_in[rows, :]
        out[...] = grad.astype(out.dtype)
        sum_one = sum_one + jnp.sum(grad * (field * factor_of(field)), axis=0, keepdims=True)
    sum_b = jnp.sum(lin[...].astype(F32), axis=0, keepdims=True)
    grad_w = tn(attn_in[...], lin[...])
    grad_o = tn(branch[...], att[...])
    first_w = grad_w[:, :512]
    second_w = jnp.concatenate([grad_o[:, :384], grad_o[:, 384:] + grad_w[:, 512:]], axis=1)
    nothing = jnp.zeros((8, 512), F32)

    def eight(row):
        return jnp.broadcast_to(row, (8, 512))

    zeros_128 = jnp.zeros((1, 128), F32)
    extra_a = {0: sum_b[:, :512], 1: sum_one[:, :512], 2: sum_two[:, :512]}
    extra_b = {
        0: jnp.concatenate([zeros_128] * 3 + [sum_b[:, 512:]], axis=1),
        1: jnp.concatenate([sum_one[:, 512:], zeros_128], axis=1),
        2: jnp.concatenate([sum_two[:, 512:], zeros_128], axis=1),
    }
    for piece in range(16):
        rows = slice(PIECE * piece, PIECE * piece + PIECE)
        for out, grads, extra in ((pack_a, first_w, extra_a), (pack_b, second_w, extra_b)):
            more = eight(extra[piece]) if piece in extra else nothing
            out[piece] = jnp.concatenate([grads[rows, :], more], axis=0).astype(BF)


def back(info, *args):
    return pl.pallas_call(
        back_kernel,
        name="attention_backward",
        in_specs=[SM] + [VM] * 17,
        out_specs=[VM] * 5,
        out_shape=[
            sds((HALF, D), F32),
            sds((HALF, D), F32),
            sds((HALF, D), BF),
            sds((16, 64, 512), BF),
            sds((16, 64, 512), BF),
        ],
        scratch_shapes=[
            pltpu.VMEM((ROWS, D), BF),
            pltpu.VMEM((ROWS, D), BF),
            pltpu.VMEM((ROWS, 640), BF),
            pltpu.VMEM((ROWS, D), F32),
        ],
        compiler_params=params(60),
        cost_estimate=cost(9 * 10**9, 24 * 10**6, 3 * 10**6),
    )(info, *args)


def wide_kernel(info, a_own, a_rec, b_own, b_rec, gate, up):
    first = info[4] == 0
    for out, in_a, in_b in ((gate, slice(0, 768), slice(0, 512)), (up, slice(1536, 2304), slice(512, 1024))):
        ours_a, theirs_a = a_own[0, :, in_a].astype(F32), a_rec[0, :, in_a].astype(F32)
        ours_b, theirs_b = b_own[0, :, in_b].astype(F32), b_rec[0, :, in_b].astype(F32)
        out[:, 0:768] = jnp.where(first, ours_a, theirs_a)
        out[:, 768:1280] = jnp.where(first, ours_b, theirs_b)
        out[:, 1280:1920] = jnp.where(first, theirs_a, ours_a)[:, 128:]
        out[:, 1920:2432] = jnp.where(first, theirs_b, ours_b)


def wide(info, a_own, a_rec, b_own, b_rec):
    block_a = pl.BlockSpec((1, PIECE, 2304), lambda p: (p, 0, 0))
    block_b = pl.BlockSpec((1, PIECE, 1536), lambda p: (p, 0, 0))
    return pl.pallas_call(
        wide_kernel,
        name="gradients_wide",
        grid=(16,),
        in_specs=[SM, block_a, block_a, block_b, block_b],
        out_specs=[
            pl.BlockSpec((PIECE, 2432), lambda p: (p, 0)),
            pl.BlockSpec((PIECE, 2432), lambda p: ((p % 4) * 4 + p // 4, 0)),
        ],
        out_shape=[sds((D, 2432), F32)] * 2,
        compiler_params=params(32),
        cost_estimate=cost(10**7, 28 * 10**6),
    )(info, a_own, a_rec, b_own, b_rec)


def tall_kernel(info, a_own, a_rec, b_own, b_rec, down):
    step = pl.program_id(0)
    first = (info[4] == 0) == (step < 10)
    tile = jnp.where(step < 10, step, step - 9)

    @pl.when(tile < 6)
    def _():
        picked = jnp.where(first, a_own[...].astype(F32), a_rec[...].astype(F32))
        down[...] = picked.reshape(D, 128).T

    @pl.when(tile >= 6)
    def _():
        picked = jnp.where(first, b_own[...].astype(F32), b_rec[...].astype(F32))
        order = [picked[4 * (q % 4) + q // 4] for q in range(16)]
        down[...] = jnp.concatenate(order, axis=0).T


def tall(info, a_own, a_rec, b_own, b_rec):
    def tile(k):
        return jnp.where(k < 10, k, k - 9)

    block_a = pl.BlockSpec((16, PIECE, 128), lambda k: (0, 0, 6 + jnp.minimum(tile(k), 5)))
    block_b = pl.BlockSpec((16, PIECE, 128), lambda k: (0, 0, 8 + jnp.maximum(tile(k) - 6, 0)))
    return pl.pallas_call(
        tall_kernel,
        name="gradients_tall",
        grid=(19,),
        in_specs=[SM, block_a, block_a, block_b, block_b],
        out_specs=pl.BlockSpec((128, D), lambda k: (k, 0)),
        out_shape=sds((2432, D), F32),
        compiler_params=params(32),
        cost_estimate=cost(10**7, 14 * 10**6),
    )(info, a_own, a_rec, b_own, b_rec)


def send(field, axis, shift=1):
    size = lax.axis_size(axis)
    return lax.ppermute(field, axis, [(i, (i + shift) % size) for i in range(size)])


def after(field, *others):
    return lax.optimization_barrier((field, *others))[0]


def by_place(place, own, rec, axis=0):
    first = place == 0
    return jnp.concatenate([jnp.where(first, own, rec), jnp.where(first, rec, own)], axis=axis)


def swapped(weight):
    return jnp.concatenate([-weight[..., HD // 2 :], weight[..., : HD // 2]], axis=-1)


def tables(is_long):
    row = jnp.arange(ROWS, dtype=jnp.int32)
    second = (row >= 512).astype(jnp.int32) * 512
    offset = jnp.where(is_long == 1, second, row // 256 * 256)
    freq_index = jnp.arange(HD // 2, dtype=F32)
    inverse = ROPE_BASE ** (-2.0 * freq_index / HD)
    angle = (row - offset).astype(F32)[:, None] * inverse[None, :]
    cosine, sine = jnp.cos(angle), jnp.sin(angle)
    return (
        jnp.concatenate([cosine] * 4, axis=1),
        jnp.concatenate([sine, sine, -sine, -sine], axis=1),
    )


def scatter_x_y(info, slots_x, slots_y):
    got_x = [slots_x[0]] + [send(slots_x[s], "x", s) for s in (1, 2, 3)]
    got_y = [slots_y[0]] + [send(slots_y[s], "y", s) for s in (1, 2, 3)]
    mid = fold(info, got_x, got_y)
    mid_x, mid_y = mid[:4], mid[4:]
    got_x = [mid_x[0]] + [send(mid_x[s], "y", s) for s in (1, 2, 3)]
    got_y = [mid_y[0]] + [send(mid_y[s], "x", s) for s in (1, 2, 3)]
    part = join(got_x, got_y)
    return add(part, send(part, "zl"))


def add(one, two):
    return (one.astype(F32) + two.astype(F32)).astype(BF)


def gather(part):
    return lax.all_gather(part, ("x", "y"), axis=0, tiled=False)


def shards(tokens, long_count, attn_gain, w_query, b_query, w_key, b_key, w_value, b_value,
           w_out, mlp_gain, w_gate, w_up, w_down, cotangent):
    at_x, at_y, at_c, at_t = (lax.axis_index(a) for a in ("x", "y", "c", "t"))
    info = jnp.stack([at_t, long_count[0], at_x, at_y, at_c]).astype(jnp.int32)
    gain_one = attn_gain.astype(F32)[None, :]
    gain_two = mlp_gain.astype(F32)[None, :]

    tok_rec = send(tokens, "t")
    half_out = lax.dynamic_slice(w_out, (at_c * SLAB, 0), (SLAB, D))
    half_out = send(after(half_out, tok_rec), "t")
    other_out = by_place(at_c, half_out, send(half_out, "c"))

    heads = w_query.reshape(D, HEADS, HD)
    heads = jnp.concatenate([heads, swapped(heads)], axis=-1).reshape(D, HEADS * 128)
    w_all = jnp.concatenate([heads, w_key, swapped(w_key), w_value, w_value], axis=1)
    bias = b_query.reshape(HEADS, HD)
    bias = jnp.concatenate([bias, swapped(bias)], axis=-1).reshape(HEADS * 128)
    b_all = jnp.concatenate([bias, b_key, swapped(b_key), b_value, b_value]).astype(F32)[None, :]
    w_cat = jnp.concatenate([w_query, w_key, jnp.zeros((D, HD), BF), w_value], axis=1)
    wo_dup = w_out.reshape(HEADS, HD, D)
    wo_dup = jnp.concatenate([wo_dup, wo_dup], axis=1).reshape(HEADS * 128, D)
    cosine, sine = tables(long_count[0])
    first_hid = at_c * STEP
    wg = lax.dynamic_slice(w_gate, (0, first_hid), (D, HID))
    wu = lax.dynamic_slice(w_up, (0, first_hid), (D, HID))
    wd = lax.dynamic_slice(w_down, (first_hid, 0), (HID, D))
    shared = (lax.iota(jnp.int32, HID) < 128) & (at_c == 1)
    wd = jnp.where(shared[:, None], jnp.zeros((), BF), wd)

    attn_in, rotated, value, stats, att_send, att_keep = attention(
        info, tokens, tok_rec, gain_one, w_all, b_all, cosine, sine
    )
    att_rec = send(att_send, "t")
    cot_rec = send(after(cotangent, half_out), "t")
    cot = by_place(at_t, cotangent, cot_rec)
    cot_other = send(cot, "c")
    g_x, g_y = turn(info, cot, cot_other)
    hidden, mlp_in = project(info, att_send, att_rec, w_out, other_out, tokens, tok_rec, gain_two)
    mlp_other = send(mlp_in, "c")
    m_x, m_y = turn(info, mlp_in, mlp_other)
    one = feed(True, mlp_in, mlp_other, cot, cot_other, m_x, m_y, g_x, wg, wu, wd, ())
    two = feed(False, mlp_in, mlp_other, cot, cot_other, m_x, m_y, g_y, wg, wu, wd, one[8:])
    out_own, out_other, dm_own, dm_other = two[8:]

    sum_one = scatter_x_y(info, one[:4], one[4:8])
    all_one = gather(sum_one)

    dm_sum = add(dm_own, send(dm_other, "c"))
    dm_rec = send(dm_sum, "t")
    out_sum = out_own.astype(F32) + send(out_other, "c").astype(F32)
    out_mine = lax.dynamic_slice(out_sum, (at_t * HALF, 0), (HALF, D))
    out_theirs = lax.dynamic_slice(out_sum, ((1 - at_t) * HALF, 0), (HALF, D)).astype(BF)
    hidden_mine = lax.dynamic_slice(hidden, (at_t * HALF, 0), (HALF, D))
    output = (hidden_mine + out_mine + send(out_theirs, "t").astype(F32)).astype(BF)

    sum_two = scatter_x_y(info, two[:4], two[4:8])
    all_two = gather(sum_two)

    grad_mid, da_own, da_send, pack_a, pack_b = back(
        info, dm_sum, dm_rec, cot, hidden, gain_two, tokens, tok_rec, gain_one, wo_dup, att_keep,
        rotated, value, stats, cosine, sine, attn_in, w_cat,
    )
    pack_send = jnp.where(at_c == 0, pack_b, pack_a)
    pack_keep = jnp.where(at_c == 0, pack_a, pack_b)
    pack = add(pack_keep, send(pack_send, "c"))
    pack = lax.psum_scatter(pack, ("x", "y"), scatter_dimension=0, tiled=True)
    pack = gather(add(pack, send(pack, "zl"))[0])

    da_rec = send(da_send, "t")
    field = tokens.astype(F32)
    factor = factor_of(field)
    normed = field * factor
    scaled = (da_own + da_rec.astype(F32)) * gain_one
    grad_tokens = grad_mid + factor * (
        scaled - normed * jnp.mean(scaled * normed, axis=-1, keepdims=True)
    )
    grad_tokens = grad_tokens.astype(BF)

    one_rec, two_rec, pack_rec = send(all_one, "c"), send(all_two, "c"), send(pack, "c")
    grad_w_gate, grad_w_up = wide(info, all_one, one_rec, all_two, two_rec)
    grad_w_down = tall(info, all_one, one_rec, all_two, two_rec)
    pack_a = jnp.where(at_c == 0, pack, pack_rec).astype(F32)
    pack_b = jnp.where(at_c == 0, pack_rec, pack).astype(F32)
    rows_a = pack_a[:, :PIECE].reshape(D, 512)
    rows_b = pack_b[:, :PIECE].reshape(D, 512)
    gains = jnp.concatenate([pack_a[1:3, PIECE], pack_b[1:3, PIECE, :384]], axis=1)
    gains = gains + send(gains, "t")
    return (
        output,
        grad_tokens,
        gains[0],
        rows_a[:, :448],
        pack_a[0, PIECE, :448],
        rows_a[:, 448:],
        pack_a[0, PIECE, 448:],
        rows_b[:, 448:],
        pack_b[0, PIECE, 448:],
        rows_b[:, :448].T,
        gains[1],
        grad_w_gate,
        grad_w_up,
        grad_w_down,
    )


def solution(mesh):
    fine = Mesh(mesh.devices.reshape(4, 2, 4, 2, 2), ("x", "zl", "y", "c", "t"))
    dp = ("x", "zl", "y", "c")
    rows, cols, split = P((*dp, "t"), None), P(None, "t"), P("t")
    down = P("t", None)
    return jax.shard_map(
        shards,
        mesh=fine,
        in_specs=(
            rows, P(dp), P(), cols, split, cols, split, cols, split, down, P(), cols, cols, down,
            rows,
        ),
        out_specs=(
            rows, rows, P(), cols, split, cols, split, cols, split, down, P(), cols, cols, down,
        ),
        check_vma=False,
    )
```

time: 1060 us -> 535 us (0.50)
  waiting for transfers between devices: 551 us -> 223 us
  blocking collectives: 281 us -> 0 us
  Pallas kernels: 0 us -> 137 us
  matrix products: 135 us -> 0 us
  starting transfers between devices: 1.12 us -> 80.6 us
    psum x1 -> x0, waiting for transfers between devices: 372 us -> none  [shards(): lax.psum((grad_w_query, grad_b_query, grad_w_key, grad_b_key, grad_w_valu...]
    psum x2 -> x0, blocking collectives: 281 us -> none  [the longest x1 274 us: shards(): lax.psum((grad_w_query, grad_b_query, grad_w_key, grad_b_key, grad_w_valu...]
    pallas_call x0 -> x13, Pallas kernels: none -> 137 us  [the longest x2 59.1 us: feed(): pl.pallas_call(functools.partial(feed_kernel, first, lanes), name='feed_f...]
    dot_general x27 -> x0, matrix products: 135 us -> none  [the longest x7 35.4 us: dot_last(): lax.dot_general(left, right, (((1,), (1,)), ((), ())), preferred_element_...]
    ppermute x0 -> x44, waiting for transfers between devices: none -> 106 us  [send(): lax.ppermute(field, axis, [(i, (i + shift) % size) for i in range(size)])]
    reduce_scatter x4 -> x0, waiting for transfers between devices: 83.4 us -> none  [the longest x1 42.1 us: shards(): lax.psum_scatter(dot_last(grad_gate, w_gate) + dot_last(grad_up, w_up), '...]
    ppermute x0 -> x44, starting transfers between devices: none -> 80.4 us  [send(): lax.ppermute(field, axis, [(i, (i + shift) % size) for i in range(size)])]
    all_gather x4 -> x3, waiting for transfers between devices: 95 us -> 117 us  [gather(): return lax.all_gather(part, ('x', 'y'), axis=0, tiled=False)]
  transfers between devices with their start and end apart: 9 -> 48, of which waited for: 7 -> 23; matrix products, arithmetic and copies ran while one was open for 6% -> 11% of each run, Pallas kernels for 0% -> 4%
where the time goes in v1:
time: 535 us; the launch traced here: 530 us
  waiting for transfers between devices  223 us (42%)
  Pallas kernels  137 us (26%)
  starting transfers between devices  80.6 us (15%)
  local copies, waits for them, and re-layouts  39.9 us (7%)
  other arithmetic  33.8 us (6%)
  between operations  15.6 us (3%)
    all_gather x3, waiting for transfers between devices, gather(): return lax.all_gather(part, ('x', 'y'), axis=0, tiled=False)  117 us
    ppermute x44, waiting for transfers between devices, send(): lax.ppermute(field, axis, [(i, (i + shift) % size) for i in range(size)])  106 us
    ppermute x44, starting transfers between devices, send(): lax.ppermute(field, axis, [(i, (i + shift) % size) for i in range(size)])  80.4 us
    pallas_call x2, Pallas kernels, feed(): pl.pallas_call(functools.partial(feed_kernel, first, lanes), name='feed_f...  59.1 us
    pallas_call x1, Pallas kernels, back(): pl.pallas_call(back_kernel, name='attention_backward', in_specs=[SM] + [V...  24.2 us
    unnamed x124, local copies, waits for them, and re-layouts  18.3 us
    pallas_call x1, Pallas kernels, wide(): pl.pallas_call(wide_kernel, name='gradients_wide', grid=(16,), in_specs=[...  14.4 us
    pallas_call x1, Pallas kernels, tall(): pl.pallas_call(tall_kernel, name='gradients_tall', grid=(19,), in_specs=[...  13.8 us
  transfers between devices with their start and end apart: 48, of which 23 were waited for; matrix products, arithmetic and copies ran while one was open for 11% of the time, Pallas kernels for 4%

profile of v1, /device:TPU:1, one launch (start us, length us, event | category | flops | bytes accessed | tf_op | source)
XLA Modules:
  0.0 529.6 jit_solution(16014312037843485332)
XLA Ops:
  7.2 4.5 collective-permute-start
  20.5 4.5 concatenate.51.w_all
  30.0 9.9 %attention_forward.1 = (bf16[768,896]{1,0:T(8,128)(2,1)S(1)}, bf16[768,1024]{1,0:T(8,128)(2,1)}, bf16[768,128]{1,0:T(8,128)(2,1)S(1)}, f32[768,128]{1,0:T(8,128)...) custom-call(s32[5]{0:T(128)S(1)} %stack.19.info, bf16[384,896]{1,0:T(8,128)(2,1)S(1)} %copy-done.2, ...), custom_call_target="tpu_custom_call" | custom-call | flops 4000000000 | bytes 12000000 | tf_op jit(solution)/shard_map/attention_forward/pallas_call | solution.py:120
  48.2 11.6 %collective-permute-done.1 = bf16[768,448]{0,1:T(8,128)(2,1)} collective-permute-done((bf16[768,448]{0,1:T(8,128)(2,1)S(1)}, bf16[768,448]{0,1:T(8,128)(2,1)}, u32[]{:S(2)}, u32[]{:S(2)}) %collective-permute-start.1) | collective-permute-done | bytes 688160 | tf_op jit(solution)/shard_map/ppermute | solution.py:487
  66.1 5.1 collective-permute-start.4
  79.0 4.8 constant_dynamic-slice_fusion
  87.3 5.1 transpose_rows.2
  93.9 4.6 transpose_rows.3
  100.0 32.4 %feed_first.1 = (bf16[4,56,1536]{2,1,0:T(8,128)(2,1)}, bf16[4,56,1536]{2,1,0:T(8,128)(2,1)}, bf16[4,56,1536]{2,1,0:T(8,128)(2,1)}, bf16[4,56,1536]{2,1,0:T(8,128...) custom-call(bf16[768,896]{1,0:T(8,128)(2,1)} %get-tuple-element.78.o, ...), custom_call_target="tpu_custom_call" | custom-call | flops 18900000768 | bytes 30000000 | tf_op jit(solution)/shard_map/feed_first/pallas_call | solution.py:242
  132.4 26.7 %feed_second.1 = (bf16[4,56,512]{2,1,0:T(8,128)(2,1)}, bf16[4,56,512]{2,1,0:T(8,128)(2,1)}, bf16[4,56,512]{2,1,0:T(8,128)(2,1)}, bf16[4,56,512]{2,1,0:T(8,128)(2...) custom-call(bf16[768,896]{1,0:T(8,128)(2,1)} %get-tuple-element.78.o, ...), custom_call_target="tpu_custom_call" | custom-call | flops 12600000512 | bytes 30000000 | tf_op jit(solution)/shard_map/feed_second/pallas_call | solution.py:242
  170.4 28.5 %collective-permute-done.10.dm_rec = bf16[768,896]{1,0:T(8,128)(2,1)} collective-permute-done((bf16[768,896]{1,0:T(8,128)(2,1)}, bf16[768,896]{1,0:T(8,128)(2,1)}, u32[]{:S(2)}, u32[]{:S(2)}) %collective-permute-start.10) | collective-permute-done | bytes 1376288 | tf_op jit(solution)/shard_map/ppermute | solution.py:487
  198.8 24.2 %attention_backward.1 = (f32[384,896]{1,0:T(8,128)}, f32[384,896]{1,0:T(8,128)}, bf16[384,896]{1,0:T(8,128)(2,1)}, bf16[16,64,512]{2,1,0:T(8,128)(2,1)}, bf16[16,64,512]{2,1,0:T(8,128)(2,1)}) custom-call(s32[5]{0:T(128)} %copy-done.16, bf16[768,896]{1,0:T(8,128)(2,1)} %add_convert_fusion.dm_own, bf16[768,896]{1,0:T(8,128)(2,1)} %collective-permute-done.10.dm_rec, ...), custom_call_target="tpu_custom_call" | custom-call | flops 8999999488 | bytes 24000000 | tf_op jit(solution)/shard_map/attention_backward/pallas_call | solution.py:398
  241.7 7.8 %collective-permute-done.20.refs_6_ = bf16[4,56,768]{2,1,0:T(8,128)(2,1)S(1)} collective-permute-done((bf16[4,56,768]{2,1,0:T(8,128)(2,1)}, bf16[4,56,768]{2,1,0:T(8,128)(2,1)S(1)}, u32[]{:S(2)}, u32[]{:S(2)}) %collective-permute-start.20) | collective-permute-done | bytes 344096 | tf_op jit(solution)/shard_map/ppermute | solution.py:487
  249.5 4.0 collective-permute-done.21.refs_7_
  253.5 11.9 %collective-permute-done.17.refs_2_ = bf16[4,56,1536]{2,1,0:T(8,128)(2,1)S(1)} collective-permute-done((bf16[4,56,1536]{2,1,0:T(8,128)(2,1)}, bf16[4,56,1536]{2,1,0:T(8,128)(2,1)S(1)}, u32[]{:S(2)}, u32[]{:S(2)}) %collective-permute-start.17) | collective-permute-done | bytes 688160 | tf_op jit(solution)/shard_map/ppermute | solution.py:487
  280.6 4.7 collective-permute-done.28
  303.1 5.9 %collective-permute-done.34.refs_6_ = bf16[4,56,1024]{2,1,0:T(8,128)(2,1)S(1)} collective-permute-done((bf16[4,56,1024]{2,1,0:T(8,128)(2,1)S(1)}, bf16[4,56,1024]{2,1,0:T(8,128)(2,1)S(1)}, u32[]{:S(2)}, u32[]{:S(2)}) %collective-permute-start.34) | collective-permute-done | bytes 458784 | tf_op jit(solution)/shard_map/ppermute | solution.py:487
  330.9 4.2 collective-permute-start.7
  340.4 36.2 %all-gather.8.cloned.1.call-done = bf16[896,2304]{1,0:T(8,128)(2,1)} async-done(((bf16[56,2304]{1,0:T(8,128)(2,1)}), bf16[896,2304]{1,0:T(8,128)(2,1)}) %all-gather.8.cloned.1.call-update) | async-done | bytes 4128784 | tf_op jit(solution)/shard_map/all_gather | solution.py:533
  378.4 3.7 convert_add_fusion
  387.4 38.2 %all-gather.10.cloned.1.call-done = bf16[896,1536]{1,0:T(8,128)(2,1)} async-done(((bf16[56,1536]{1,0:T(8,128)(2,1)}), bf16[896,1536]{1,0:T(8,128)(2,1)}) %all-gather.10.cloned.1.call-update) | async-done | bytes 2752528 | tf_op jit(solution)/shard_map/all_gather | solution.py:533
  426.8 42.3 %all-gather.6.cloned.1.call-done = bf16[16,64,512]{2,1,0:T(8,128)(2,1)} async-done(((bf16[1,64,512]{2,1,0:T(8,128)(2,1)}), bf16[16,64,512]{2,1,0:T(8,128)(2,1)}) %all-gather.6.cloned.1.call-update) | async-done | bytes 1048592 | tf_op jit(solution)/shard_map/all_gather | solution.py:533
  494.4 14.4 %gradients_wide.1 = (f32[896,2432]{1,0:T(8,128)}, f32[896,2432]{1,0:T(8,128)}) custom-call(s32[5]{0:T(128)S(1)} %copy-done.17, bf16[16,56,2304]{2,1,0:T(8,128)(2,1)S(1)} %bitcast.41, bf16[16,56,2304]{2,1,0:T(8,128)(2,1)} %collective-permute-done.29.a_rec, bf16[16,56,1536]{2,1,0:T(8,128)(2,1)S(1)} %bitcast.44, bf16[16,56,1536]{2,1,0:T(8,128)(2,1)} %collective-permute-done.43.b_rec), custom_call_target="tpu_custom_call" | custom-call | flops 10000000 | bytes 28000000 | tf_op jit(solution)/shard_map/gradients_wide/pallas_call | solution.py:435
  508.8 13.8 %gradients_tall.1 = f32[2432,896]{1,0:T(8,128)} custom-call(s32[5]{0:T(128)S(1)} %copy-done.17, bf16[16,56,2304]{2,1,0:T(8,128)(2,1)S(1)} %bitcast.42, bf16[16,56,2304]{2,1,0:T(8,128)(2,1)} %collective-permute-done.29.a_rec, bf16[16,56,1536]{2,1,0:T(8,128)(2,1)S(1)} %bitcast.45, bf16[16,56,1536]{2,1,0:T(8,128)(2,1)} %collective-permute-done.43.b_rec), custom_call_target="tpu_custom_call" | custom-call | flops 10000000 | bytes 14000000 | tf_op jit(solution)/shard_map/gradients_tall/pallas_call | solution.py:473
  (273 shorter events, 165.0 us)
Async XLA Ops:
  7.2 327.9 %reduce-scatter.4.cloned.1.call-start = ((), (), s32[]{:S(2)}) async-start(), calls=%async_computation.4 | async-start | bytes 1114112
  7.2 20.7 %collective-permute-start = (bf16[384,896]{1,0:T(8,128)(2,1)}, bf16[384,896]{1,0:T(8,128)(2,1)S(1)}, u32[]{:S(2)}, u32[]{:S(2)}) collective-permute-start(bf16[384,896]{1,0:T(8,128)(2,1)} %tok_own.5), channel_id=1, source_target_pairs={{0,1},{1,0},{2,3},{3,2},{4,5},{5,4},{6,7},{7,6},{8,9},{9,8},{10,11... | collective-permute-start | bytes 2064392 | tf_op jit(solution)/shard_map/ppermute | solution.py:487
  27.9 16.4 %collective-permute-start.2 = (bf16[224,896]{1,0:T(8,128)(2,1)}, bf16[224,896]{1,0:T(8,128)(2,1)}, u32[]{:S(2)}, u32[]{:S(2)}) collective-permute-start(bf16[224,896]{1,0:T(8,128)(2,1)} %constant_dynamic-slice_fusion.2), channel_id=1, source_target_pairs={{0,1},{1,0},{2,3},{3,2},{4,5},{5,4},{6,7},{7,6},{8,9},{9,8},{10,11... | collective-permute-start | bytes 1204232 | tf_op jit(solution)/shard_map/ppermute | solution.py:487
  43.0 16.8 %collective-permute-start.1 = (bf16[768,448]{0,1:T(8,128)(2,1)S(1)}, bf16[768,448]{0,1:T(8,128)(2,1)}, u32[]{:S(2)}, u32[]{:S(2)}) collective-permute-start(bf16[768,448]{0,1:T(8,128)(2,1)S(1)} %copy.79), channel_id=1, source_target_pairs={{0,1},{1,0},{2,3},{3,2},{4,5},{5,4},{6,7},{7,6},{8,9},{9,8},{10,11... | collective-permute-start | bytes 2064392 | tf_op jit(solution)/shard_map/ppermute | solution.py:487
  44.3 16.9 %collective-permute-start.3 = (bf16[224,896]{1,0:T(8,128)(2,1)}, bf16[224,896]{1,0:T(8,128)(2,1)}, u32[]{:S(2)}, u32[]{:S(2)}) collective-permute-start(bf16[224,896]{1,0:T(8,128)(2,1)} %collective-permute-done.2), channel_id=1, source_target_pairs={{0,2},{2,0},{1,3},{3,1},{4,6},{6,4},{5,7},{7,5},{8,10},{10,8},{9,1... | collective-permute-start | bytes 1204232 | tf_op jit(solution)/shard_map/ppermute | solution.py:487
  45.8 28.7 %collective-permute-start.5 = (bf16[384,896]{1,0:T(8,128)(2,1)}, bf16[384,896]{1,0:T(8,128)(2,1)}, u32[]{:S(2)}, u32[]{:S(2)}) collective-permute-start(bf16[384,896]{1,0:T(8,128)(2,1)} %param.29), channel_id=1, source_target_pairs={{0,1},{1,0},{2,3},{3,2},{4,5},{5,4},{6,7},{7,6},{8,9},{9,8},{10,11... | collective-permute-start | bytes 2064392 | tf_op jit(solution)/shard_map/ppermute | solution.py:487
  66.1 21.2 %collective-permute-start.4 = (bf16[768,896]{1,0:T(8,128)(2,1)}, bf16[768,896]{1,0:T(8,128)(2,1)S(1)}, u32[]{:S(2)}, u32[]{:S(2)}) collective-permute-start(bf16[768,896]{1,0:T(8,128)(2,1)} %get-tuple-element.78.own.m_own), channel_id=1, source_target_pairs={{0,2},{2,0},{1,3},{3,1},{4,6},{6,4},{5,7},{7,5},{8,10},{10,8},{9,1... | collective-permute-start | bytes 4128776 | tf_op jit(solution)/shard_map/ppermute | solution.py:487
  75.9 18.0 %collective-permute-start.6 = (bf16[768,896]{1,0:T(8,128)(2,1)S(1)}, bf16[768,896]{1,0:T(8,128)(2,1)}, u32[]{:S(2)}, u32[]{:S(2)}) collective-permute-start(bf16[768,896]{1,0:T(8,128)(2,1)S(1)} %pad_maximum_fusion.2.own.g_own.cot), channel_id=1, source_target_pairs={{0,2},{2,0},{1,3},{3,1},{4,6},{6,4},{5,7},{7,5},{8,10},{10,8},{9,1... | collective-permute-start | bytes 4128776 | tf_op jit(solution)/shard_map/ppermute | solution.py:487
  165.4 33.5 %collective-permute-start.10 = (bf16[768,896]{1,0:T(8,128)(2,1)}, bf16[768,896]{1,0:T(8,128)(2,1)}, u32[]{:S(2)}, u32[]{:S(2)}) collective-permute-start(bf16[768,896]{1,0:T(8,128)(2,1)} %add_convert_fusion.dm_own), channel_id=1, source_target_pairs={{0,1},{1,0},{2,3},{3,2},{4,5},{5,4},{6,7},{7,6},{8,9},{9,8},{10,11... | collective-permute-start | bytes 4128776 | tf_op jit(solution)/shard_map/ppermute | solution.py:487
  229.3 147.3 %all-gather.8.cloned.1.call-start = ((), (), s32[]{:S(2)}) async-start(), calls=%async_computation.2 | async-start | bytes 4386816 | tf_op jit(solution)/shard_map/all_gather | solution.py:533
  230.8 22.8 %collective-permute-start.16 = (bf16[4,56,1536]{2,1,0:T(8,128)(2,1)}, bf16[4,56,1536]{2,1,0:T(8,128)(2,1)S(1)}, u32[]{:S(2)}, u32[]{:S(2)}) collective-permute-start(bf16[4,56,1536]{2,1,0:T(8,128)(2,1)} %get-tuple-element.103), channel_id=1, source_target_pairs={{0,32},{32,64},{64,96},{96,0},{1,33},{33,65},{65,97},{97,1},{2,34}... | collective-permute-start | bytes 2064392 | tf_op jit(solution)/shard_map/ppermute | solution.py:487
  232.0 33.4 %collective-permute-start.17 = (bf16[4,56,1536]{2,1,0:T(8,128)(2,1)}, bf16[4,56,1536]{2,1,0:T(8,128)(2,1)S(1)}, u32[]{:S(2)}, u32[]{:S(2)}) collective-permute-start(bf16[4,56,1536]{2,1,0:T(8,128)(2,1)} %get-tuple-element.104), channel_id=1, source_target_pairs={{0,64},{32,96},{64,0},{96,32},{1,65},{33,97},{65,1},{97,33},{2,66}... | collective-permute-start | bytes 2064392 | tf_op jit(solution)/shard_map/ppermute | solution.py:487
  234.4 31.0 %collective-permute-start.18 = (bf16[4,56,1536]{2,1,0:T(8,128)(2,1)}, bf16[4,56,1536]{2,1,0:T(8,128)(2,1)S(1)}, u32[]{:S(2)}, u32[]{:S(2)}) collective-permute-start(bf16[4,56,1536]{2,1,0:T(8,128)(2,1)} %get-tuple-element.105), channel_id=1, source_target_pairs={{0,96},{32,0},{64,32},{96,64},{1,97},{33,1},{65,33},{97,65},{2,98}... | collective-permute-start | bytes 2064392 | tf_op jit(solution)/shard_map/ppermute | solution.py:487
  235.6 13.9 %collective-permute-start.20 = (bf16[4,56,768]{2,1,0:T(8,128)(2,1)}, bf16[4,56,768]{2,1,0:T(8,128)(2,1)S(1)}, u32[]{:S(2)}, u32[]{:S(2)}) collective-permute-start(bf16[4,56,768]{2,1,0:T(8,128)(2,1)} %get-tuple-element.108), channel_id=1, source_target_pairs={{0,8},{4,12},{8,0},{12,4},{1,9},{5,13},{9,1},{13,5},{2,10},{6,14},... | collective-permute-start | bytes 1032200 | tf_op jit(solution)/shard_map/ppermute | solution.py:487
  286.1 139.5 %all-gather.10.cloned.1.call-start = ((), (), s32[]{:S(2)}) async-start(), calls=%async_computation.3 | async-start | bytes 2924544 | tf_op jit(solution)/shard_map/all_gather | solution.py:533
  286.3 16.8 %collective-permute-start.33 = (bf16[4,56,1024]{2,1,0:T(8,128)(2,1)S(1)}, bf16[4,56,1024]{2,1,0:T(8,128)(2,1)S(1)}, u32[]{:S(2)}, u32[]{:S(2)}) collective-permute-start(bf16[4,56,1024]{2,1,0:T(8,128)(2,1)S(1)} %copy-done.53), channel_id=1, source_target_pairs={{0,4},{4,8},{8,12},{12,0},{1,5},{5,9},{9,13},{13,1},{2,6},{6,10},{... | collective-permute-start | bytes 1376264 | tf_op jit(solution)/shard_map/ppermute | solution.py:487
  289.5 19.6 %collective-permute-start.34 = (bf16[4,56,1024]{2,1,0:T(8,128)(2,1)S(1)}, bf16[4,56,1024]{2,1,0:T(8,128)(2,1)S(1)}, u32[]{:S(2)}, u32[]{:S(2)}) collective-permute-start(bf16[4,56,1024]{2,1,0:T(8,128)(2,1)S(1)} %copy-done.52), channel_id=1, source_target_pairs={{0,8},{4,12},{8,0},{12,4},{1,9},{5,13},{9,1},{13,5},{2,10},{6,14},... | collective-permute-start | bytes 1376264 | tf_op jit(solution)/shard_map/ppermute | solution.py:487
  290.6 19.7 %collective-permute-start.35 = (bf16[4,56,1024]{2,1,0:T(8,128)(2,1)S(1)}, bf16[4,56,1024]{2,1,0:T(8,128)(2,1)S(1)}, u32[]{:S(2)}, u32[]{:S(2)}) collective-permute-start(bf16[4,56,1024]{2,1,0:T(8,128)(2,1)S(1)} %copy-done.51), channel_id=1, source_target_pairs={{0,12},{4,0},{8,4},{12,8},{1,13},{5,1},{9,5},{13,9},{2,14},{6,2},{... | collective-permute-start | bytes 1376264 | tf_op jit(solution)/shard_map/ppermute | solution.py:487
  330.8 138.3 %all-gather.6.cloned.1.call-start = ((), (), s32[]{:S(2)}) async-start(), calls=%async_computation.1 | async-start | bytes 1114112 | tf_op jit(solution)/shard_map/all_gather | solution.py:533
  330.9 46.4 %collective-permute-start.7 = (bf16[768,896]{1,0:T(8,128)(2,1)S(1)}, bf16[768,896]{1,0:T(8,128)(2,1)S(1)}, u32[]{:S(2)}, u32[]{:S(2)}) collective-permute-start(bf16[768,896]{1,0:T(8,128)(2,1)S(1)} %copy-done.50), channel_id=1, source_target_pairs={{0,2},{2,0},{1,3},{3,1},{4,6},{6,4},{5,7},{7,5},{8,10},{10,8},{9,1... | collective-permute-start | bytes 4128776 | tf_op jit(solution)/shard_map/ppermute | solution.py:487
  376.6 115.6 %collective-permute-start.29 = (bf16[16,56,2304]{2,1,0:T(8,128)(2,1)}, bf16[16,56,2304]{2,1,0:T(8,128)(2,1)}, u32[]{:S(2)}, u32[]{:S(2)}) collective-permute-start(bf16[16,56,2304]{2,1,0:T(8,128)(2,1)} %bitcast.40), channel_id=1, source_target_pairs={{0,2},{2,0},{1,3},{3,1},{4,6},{6,4},{5,7},{7,5},{8,10},{10,8},{9,1... | collective-permute-start | bytes 12386312 | tf_op jit(solution)/shard_map/ppermute | solution.py:487
  384.4 86.8 %collective-permute-start.8 = (bf16[384,896]{1,0:T(8,128)(2,1)}, bf16[384,896]{1,0:T(8,128)(2,1)}, u32[]{:S(2)}, u32[]{:S(2)}) collective-permute-start(bf16[384,896]{1,0:T(8,128)(2,1)} %dynamic-slice_convert_fusion), channel_id=1, source_target_pairs={{0,1},{1,0},{2,3},{3,2},{4,5},{5,4},{6,7},{7,6},{8,9},{9,8},{10,11... | collective-permute-start | bytes 2064392 | tf_op jit(solution)/shard_map/ppermute | solution.py:487
  387.3 86.5 %collective-permute-start.11 = (bf16[384,896]{1,0:T(8,128)(2,1)}, bf16[384,896]{1,0:T(8,128)(2,1)}, u32[]{:S(2)}, u32[]{:S(2)}) collective-permute-start(bf16[384,896]{1,0:T(8,128)(2,1)} %get-tuple-element.99), channel_id=1, source_target_pairs={{0,1},{1,0},{2,3},{3,2},{4,5},{5,4},{6,7},{7,6},{8,9},{9,8},{10,11... | collective-permute-start | bytes 2064392 | tf_op jit(solution)/shard_map/ppermute | solution.py:487
  425.6 66.6 %collective-permute-start.43 = (bf16[16,56,1536]{2,1,0:T(8,128)(2,1)}, bf16[16,56,1536]{2,1,0:T(8,128)(2,1)}, u32[]{:S(2)}, u32[]{:S(2)}) collective-permute-start(bf16[16,56,1536]{2,1,0:T(8,128)(2,1)} %bitcast.43), channel_id=1, source_target_pairs={{0,2},{2,0},{1,3},{3,1},{4,6},{6,4},{5,7},{7,5},{8,10},{10,8},{9,1... | collective-permute-start | bytes 8257544 | tf_op jit(solution)/shard_map/ppermute | solution.py:487
  (81 other events, 1047.1 us)
Sparse Core Ops, SparseCore 0:
  229.5 91.6 reduce-scatter.3
  324.2 52.3 all-gather.7
  379.6 45.9 all-gather.9
  428.4 40.6 all-gather.5
